TPU v7x, 32 devices: a whole 2x2x4 slice. The times are simulated.
32 devices in a mesh: row: 16 (over z, x, core), feat: 2 (over y).
Axes of the slice: x: 2, y: 2, z: 4, core: 2. Of those that a mesh axis runs over, the one named last changes fastest.
Arguments:
- vectors: bfloat16 [40960, 1024], P('row', 'feat')
- rotation: bfloat16 [1024, 1024], P('feat')
- codes: int32 [40960, 64], P('row', 'feat'), may hold values from 0 to 255
- live_rows: int32 [16], P('row'), may hold values from 640 to 2560
Outputs:
- centroids: float32 [256, 1024], P('row', 'feat')
- grad_t: float32 [1024, 1024], P('row', 'feat')
All inputs are finite; a program needn't handle non-finite values.
Results may differ from a plain program's by a relative error of at most 0.00094.
Values may be sent and summed in bfloat16 or wider, within the bound.
A program may use at most 128 MiB of HBM per device.

v0:
```python
import math

import jax
import jax.numpy as jnp
from jax import lax
from jax.sharding import PartitionSpec as P

K = 256


def make_hot(code_block, keeper):
    kinds = jnp.arange(K, dtype=jnp.int32)
    return (code_block[:, :, None] == kinds[None, None, :]).astype(jnp.bfloat16) * keeper[
        :, None, None
    ]


def rebuild(hot, table_part, groups, depth):
    rows = hot.shape[0]
    shaped = table_part.reshape(K, groups, depth)
    joined = jnp.einsum("nmk,kmd->nmd", hot, shaped, preferred_element_type=jnp.float32)
    return joined.reshape(rows, groups * depth).astype(jnp.bfloat16)


def blocked_sums(hot, rotated, groups, depth):
    rows = hot.shape[0]
    step_rows = math.gcd(rows, 512)
    turns = rows // step_rows

    def add_block(index, total):
        hot_block = lax.dynamic_slice_in_dim(hot, index * step_rows, step_rows, 0).astype(
            jnp.float32
        )
        rot_block = lax.dynamic_slice_in_dim(rotated, index * step_rows, step_rows, 0).reshape(
            step_rows, groups, depth
        )
        return total + jnp.einsum(
            "nmk,nmd->kmd", hot_block, rot_block, precision=lax.Precision.HIGHEST
        )

    start = jnp.zeros((K, groups, depth), jnp.float32)
    return lax.fori_loop(0, turns, add_block, start).reshape(K, groups * depth)


def shards(vectors, rotation, codes, live_rows):
    rows = vectors.shape[0]
    local = vectors.shape[1]
    groups = codes.shape[1]
    depth = local // groups
    keeper = (jnp.arange(rows, dtype=jnp.int32) < live_rows[0]).astype(jnp.bfloat16)
    hot = make_hot(codes, keeper)
    counts = jnp.sum(hot, axis=0, dtype=jnp.float32).T
    columns = lax.all_to_all(rotation, "feat", split_axis=1, concat_axis=0, tiled=True)
    block = columns
    rotated = jnp.dot(
        lax.all_gather(vectors, "feat", axis=1, tiled=True),
        block,
        preferred_element_type=jnp.float32,
    )
    sums = blocked_sums(hot, rotated, groups, depth)
    share_sums, share_counts = (
        lax.psum_scatter(sums, "row", scatter_dimension=0, tiled=True),
        lax.psum_scatter(counts, "row", scatter_dimension=0, tiled=True),
    )
    centroids = share_sums / (jnp.repeat(share_counts, depth, axis=1) + 1.0)
    table = lax.all_gather(centroids.astype(jnp.bfloat16), "row", axis=0, tiled=True)
    local_recon = rebuild(hot, table, groups, depth)
    recon = lax.all_gather(local_recon, "feat", axis=1, tiled=True)
    inverse = 1.0 / (rows * lax.axis_size("row"))
    block = recon
    product = lax.dot_general(
        block, vectors, (((0,), (0,)), ((), ())), preferred_element_type=jnp.float32
    )
    grad_t = lax.psum_scatter(product * inverse, "row", scatter_dimension=0, tiled=True)
    return (centroids, grad_t)


def solution(mesh):
    return jax.shard_map(
        shards,
        mesh=mesh,
        in_specs=(P("row", "feat"), P("feat", None), P("row", "feat"), P("row")),
        out_specs=(P("row", "feat"), P("row", "feat")),
        check_vma=False,
    )
```

profile of v0, /device:TPU:0, one launch (start us, length us, event | category | flops | bytes accessed | tf_op | source)
XLA Modules:
  0.0 365.9 jit_solution(13745441761756763513)
XLA Ops:
  8.0 0.0 all-gather.3.cloned.1.call-start
  8.0 0.7 all-gather.3.cloned.1.call-update
  8.7 2.3 copy.29
  11.0 4.2 %all-to-all-start = ((bf16[512,2,512]{0,2,1:T(8,128)(2,1)}), bf16[512,2,512]{0,2,1:T(8,128)(2,1)S(1)}, u32[]{:S(2)}, u32[]{:S(2)}) async-start(bf16[512,2,512]{0,2,1:T(8,128)(2,1)} %bitcast), calls=%async_computation | async-start | bytes 2097152 | tf_op jit(solution)/shard_map/all_to_all | solution.py:53
  15.3 0.0 reduce-scatter.12.cloned.1.call-start
  15.9 21.3 %convert_reduce_fusion = f32[32,256]{1,0:T(8,128)S(1)} fusion(s32[2560,32]{0,1:T(8,128)} %param.8, bf16[2560]{0:T(1024)(128)(2,1)S(1)} %fusion.17), kind=kLoop, calls=%fused_computation.6 | loop fusion | flops 83877888 | bytes 365568 | tf_op jit(solution)/shard_map/reduce_sum | solution.py:52
  37.2 0.8 copy.38
  38.0 0.0 reduce-scatter.12.cloned.1.call-update
  38.0 0.0 reduce-scatter.10.cloned.1.call-start
  38.1 18.0 %fusion.9 = bf16[2560,32,256]{2,0,1:T(8,128)(2,1)} fusion(s32[2560,32]{0,1:T(8,128)} %param.8, bf16[2560]{0:T(1024)(128)(2,1)S(1)} %fusion.17), kind=kLoop, calls=%fused_computation.8 | loop fusion | flops 41943040 | bytes 42275840 | tf_op jit(solution)/shard_map/mul | solution.py:13
  56.1 0.0 all-to-all-done
  56.1 0.5 copy.30
  56.7 29.5 %all-gather.3.cloned.1.call-done = bf16[2560,1024]{1,0:T(8,128)(2,1)} async-done(((bf16[2560,512]{1,0:T(8,128)(2,1)}), bf16[2560,1024]{1,0:T(8,128)(2,1)}) %all-gather.3.cloned.1.call-update) | async-done | bytes 5242896 | tf_op jit(solution)/shard_map/all_gather | solution.py:56
  86.1 7.2 %fusion.20 = f32[2560,512]{0,1:T(8,128)} fusion(bf16[2560,1024]{1,0:T(8,128)(2,1)} %all-gather.3.cloned.1.call-done, bf16[1024,512]{1,0:T(8,128)(2,1)S(1)} %bitcast.35), kind=kOutput, calls=%fused_computation.19 | convolution fusion | flops 2684354560 | bytes 11534336 | tf_op jit(solution)/shard_map/dot_general | solution.py:55
  93.3 0.0 copy-start.1
  93.3 35.6 %while.14 = (s32[]{:T(128)}, f32[256,32,16]{0,2,1:T(8,128)S(1)}, f32[2560,512]{0,1:T(8,128)}, bf16[2560,32,256]{2,0,1:T(8,128)(2,1)}, s32[]{:T(128)}, /*index=5*/s32[]{:T(128)}, s32[]{:T(128)}, s32[]{:T(128)}) while((s32[]{:T(128)}, f32[256,32,16]{0,2,1:T(8,128)S(1)}, f32[2560,512]{0,1:T(8,128)}, bf16[2560,32,256]{2,0,1:T(8,128)(2,1)}, ...), condition=%wide.region_1.0_spmd.clone, body=%wide.region_0.0_spmd.clone.sunk | while | flops 805568512 | bytes 12583069 | solution.py:42
  93.3 1.3 constant_dynamic-slice_fusion.2
  94.6 5.8 %fusion.35 = f32[256,32,16]{0,2,1:T(8,128)S(1)} fusion(f32[512,32,16]{0,2,1:T(8,128)S(1)} %bitcast.31, bf16[2560,32,256]{2,0,1:T(8,128)(2,1)} %get-tuple-element.179, s32[]{:T(128)S(6)} %select_n.10, f32[256,32,16]{0,2,1:T(8,128)S(1)} %get-tuple-element.169, pred[]{:T(512)S(6)} %compare.3), kind=kOutput, calls=%fused_computation.3.clone.1 | convolution fusion | flops 805568512 | bytes 10485765 | tf_op jit(solution)/shard_map/while/body/eval_jaxpr/nmk,nmd->kmd/dot_general | solution.py:37
  100.5 1.3 constant_dynamic-slice_fusion.2
  101.8 5.8 %fusion.35 = f32[256,32,16]{0,2,1:T(8,128)S(1)} fusion(f32[512,32,16]{0,2,1:T(8,128)S(1)} %bitcast.31, bf16[2560,32,256]{2,0,1:T(8,128)(2,1)} %get-tuple-element.179, s32[]{:T(128)S(6)} %select_n.10, f32[256,32,16]{0,2,1:T(8,128)S(1)} %get-tuple-element.169, pred[]{:T(512)S(6)} %compare.3), kind=kOutput, calls=%fused_computation.3.clone.1 | convolution fusion | flops 805568512 | bytes 10485765 | tf_op jit(solution)/shard_map/while/body/eval_jaxpr/nmk,nmd->kmd/dot_general | solution.py:37
  107.6 1.3 constant_dynamic-slice_fusion.2
  108.9 5.8 %fusion.35 = f32[256,32,16]{0,2,1:T(8,128)S(1)} fusion(f32[512,32,16]{0,2,1:T(8,128)S(1)} %bitcast.31, bf16[2560,32,256]{2,0,1:T(8,128)(2,1)} %get-tuple-element.179, s32[]{:T(128)S(6)} %select_n.10, f32[256,32,16]{0,2,1:T(8,128)S(1)} %get-tuple-element.169, pred[]{:T(512)S(6)} %compare.3), kind=kOutput, calls=%fused_computation.3.clone.1 | convolution fusion | flops 805568512 | bytes 10485765 | tf_op jit(solution)/shard_map/while/body/eval_jaxpr/nmk,nmd->kmd/dot_general | solution.py:37
  114.7 1.3 constant_dynamic-slice_fusion.2
  116.0 5.8 %fusion.35 = f32[256,32,16]{0,2,1:T(8,128)S(1)} fusion(f32[512,32,16]{0,2,1:T(8,128)S(1)} %bitcast.31, bf16[2560,32,256]{2,0,1:T(8,128)(2,1)} %get-tuple-element.179, s32[]{:T(128)S(6)} %select_n.10, f32[256,32,16]{0,2,1:T(8,128)S(1)} %get-tuple-element.169, pred[]{:T(512)S(6)} %compare.3), kind=kOutput, calls=%fused_computation.3.clone.1 | convolution fusion | flops 805568512 | bytes 10485765 | tf_op jit(solution)/shard_map/while/body/eval_jaxpr/nmk,nmd->kmd/dot_general | solution.py:37
  121.8 1.3 constant_dynamic-slice_fusion.2
  123.1 5.8 %fusion.35 = f32[256,32,16]{0,2,1:T(8,128)S(1)} fusion(f32[512,32,16]{0,2,1:T(8,128)S(1)} %bitcast.31, bf16[2560,32,256]{2,0,1:T(8,128)(2,1)} %get-tuple-element.179, s32[]{:T(128)S(6)} %select_n.10, f32[256,32,16]{0,2,1:T(8,128)S(1)} %get-tuple-element.169, pred[]{:T(512)S(6)} %compare.3), kind=kOutput, calls=%fused_computation.3.clone.1 | convolution fusion | flops 805568512 | bytes 10485765 | tf_op jit(solution)/shard_map/while/body/eval_jaxpr/nmk,nmd->kmd/dot_general | solution.py:37
  128.9 1.0 copy.36
  129.9 0.0 reduce-scatter.10.cloned.1.call-update
  129.9 0.0 all-gather.5.cloned.1.call-start
  130.0 0.0 reduce-scatter.12.cloned.1.call-done
  130.0 0.7 broadcast_add_fusion
  130.7 0.1 broadcast_in_dim.10
  130.8 0.2 add.49
  131.0 55.3 %reduce-scatter.10.cloned.1.call-done = f32[16,512]{1,0:T(8,128)} async-done(((f32[256,512]{1,0:T(8,128)}), f32[16,512]{1,0:T(8,128)}) %reduce-scatter.10.cloned.1.call-update) | async-done | bytes 32784 | tf_op jit(solution)/shard_map/reduce_scatter | solution.py:62
  186.3 1.4 fusion.19
  187.7 20.1 %all_gather.10 = bf16[256,512]{1,0:T(8,128)(2,1)S(1)} all-gather(bf16[16,512]{1,0:T(8,128)(2,1)S(1)} %get-tuple-element.133), channel_id=1, replica_groups=mesh['row'=16,'feat'=2] {'row'}, dimensions={0}, use_global_device_ids=true | all-gather | bytes 278528 | tf_op jit(solution)/shard_map/all_gather | solution.py:66
  207.8 0.1 copy.34
  208.0 0.0 copy-done.1
  208.0 0.0 copy-start
  208.0 16.1 %fusion.14 = bf16[32,16,2560]{2,1,0:T(8,128)(2,1)} fusion(bf16[256,32,16]{0,2,1:T(8,128)(2,1)S(1)} %bitcast.36, s32[2560,32]{0,1:T(8,128)S(1)} %copy-done.1, bf16[2560]{0:T(1024)(128)(2,1)S(1)} %fusion.17), kind=kOutput, calls=%fused_computation.12 | convolution fusion | flops 714342400 | bytes 3216384 | tf_op jit(solution)/shard_map/nmk,kmd->nmd/dot_general | solution.py:21
  224.0 0.0 all-gather.5.cloned.1.call-update
  224.1 0.0 reduce-scatter.8.cloned.1.call-start
  224.1 65.9 %all-gather.5.cloned.1.call-done = bf16[2560,1024]{0,1:T(8,128)(2,1)} async-done(((bf16[2560,512]{0,1:T(8,128)(2,1)}), bf16[2560,1024]{0,1:T(8,128)(2,1)}) %all-gather.5.cloned.1.call-update) | async-done | bytes 5242896 | tf_op jit(solution)/shard_map/all_gather | solution.py:68
  290.0 0.0 copy-done
  290.0 6.7 %convolution_multiply_fusion = f32[1024,512]{1,0:T(8,128)} fusion(bf16[2560,1024]{0,1:T(8,128)(2,1)} %all-gather.5.cloned.1.call-done, bf16[2560,512]{1,0:T(8,128)(2,1)S(1)} %copy-done), kind=kOutput, calls=%fused_computation.13 | convolution fusion | flops 2684878848 | bytes 9961472 | tf_op jit(solution)/shard_map/dot_general | solution.py:71
  296.7 0.0 reduce-scatter.8.cloned.1.call-update
  296.7 61.6 %reduce-scatter.8.cloned.1.call-done = f32[64,512]{1,0:T(8,128)} async-done(((f32[1024,512]{1,0:T(8,128)}), f32[64,512]{1,0:T(8,128)}) %reduce-scatter.8.cloned.1.call-update) | async-done | bytes 131088 | tf_op jit(solution)/shard_map/reduce_scatter | solution.py:74
  (2 shorter events, 0.0 us)
Async XLA Ops:
  8.0 78.1 %all-gather.3.cloned.1.call-start = ((), (), s32[]{:S(2)}) async-start(), calls=%async_computation.4 | async-start | bytes 7864320 | tf_op jit(solution)/shard_map/all_gather | solution.py:56
  11.0 45.1 %all-to-all-start = ((bf16[512,2,512]{0,2,1:T(8,128)(2,1)}), bf16[512,2,512]{0,2,1:T(8,128)(2,1)S(1)}, u32[]{:S(2)}, u32[]{:S(2)}) async-start(bf16[512,2,512]{0,2,1:T(8,128)(2,1)} %bitcast), calls=%async_computation | async-start | bytes 2097152 | tf_op jit(solution)/shard_map/all_to_all | solution.py:53
  15.3 114.7 %reduce-scatter.12.cloned.1.call-start = ((), (), s32[]{:S(2)}) async-start(), calls=%async_computation.8 | async-start | bytes 139264 | tf_op jit(solution)/shard_map/reduce_scatter | solution.py:63
  38.0 148.3 %reduce-scatter.10.cloned.1.call-start = ((), (), s32[]{:S(2)}) async-start(), calls=%async_computation.7 | async-start | bytes 557056 | tf_op jit(solution)/shard_map/reduce_scatter | solution.py:62
  93.3 114.7 %copy-start.1 = (s32[2560,32]{0,1:T(8,128)S(1)}, s32[2560,32]{0,1:T(8,128)}, u32[]{:S(2)}) copy-start(s32[2560,32]{0,1:T(8,128)} %param.8) | copy-start | bytes 983044
  129.9 160.1 %all-gather.5.cloned.1.call-start = ((), (), s32[]{:S(2)}) async-start(), calls=%async_computation.5 | async-start | bytes 7864320 | tf_op jit(solution)/shard_map/all_gather | solution.py:68
  208.0 82.1 %copy-start = (bf16[2560,512]{1,0:T(8,128)(2,1)S(1)}, bf16[2560,512]{1,0:T(8,128)(2,1)}, u32[]{:S(2)}) copy-start(bf16[2560,512]{1,0:T(8,128)(2,1)} %param.6) | copy-start | bytes 7864324
  224.1 134.3 %reduce-scatter.8.cloned.1.call-start = ((), (), s32[]{:S(2)}) async-start(), calls=%async_computation.6 | async-start | bytes 2228224 | tf_op jit(solution)/shard_map/reduce_scatter | solution.py:74
Sparse Core Ops, SparseCore 0:
  10.4 75.7 all-gather.2
  224.2 65.7 all-gather.4
Sparse Core Ops, SparseCore 1:
  38.1 57.6 reduce-scatter.11
  130.0 56.2 reduce-scatter.9
  296.8 61.5 reduce-scatter.7
where the time goes:
time: 367 us; the launch traced here: 366 us
  waiting for transfers between devices  213 us (58%)
  matrix products  58.9 us (16%)
  other arithmetic  41.4 us (11%)
  blocking collectives  20.1 us (5%)
  between operations  16.4 us (4%)
  local copies, waits for them, and re-layouts  11.6 us (3%)
  starting transfers between devices  4.4 us (1%)
    all_gather x1, waiting for transfers between devices, shards(): recon = lax.all_gather(local_recon, 'feat', axis=1, tiled=True)  65.9 us
    reduce_scatter x1, waiting for transfers between devices, shards(): lax.psum_scatter(product * inverse, 'row', scatter_dimension=0, tiled=True)  61.6 us
    reduce_scatter x1, waiting for transfers between devices, shards(): lax.psum_scatter(sums, 'row', scatter_dimension=0, tiled=True)  55.3 us
    all_gather x1, waiting for transfers between devices, shards(): lax.all_gather(vectors, 'feat', axis=1, tiled=True)  29.5 us
    dot_general x5, matrix products, add_block(): jnp.einsum('nmk,nmd->kmd', hot_block, rot_block, precision=lax.Precision....  29 us
    reduce_sum x1, other arithmetic, shards(): counts = jnp.sum(hot, axis=0, dtype=jnp.float32).T  21.3 us
    all_gather x1, blocking collectives, shards(): lax.all_gather(centroids.astype(jnp.bfloat16), 'row', axis=0, tiled=True)  20.1 us
    mul x1, other arithmetic, make_hot(): (code_block[:, :, None] == kinds[None, None, :]).astype(jnp.bfloat16)  18 us
  transfers between devices with their start and end apart: 6, of which 4 were waited for; matrix products, arithmetic and copies ran while one was open for 24% of the time, Pallas kernels for 0%

commit v1 on v0

v1 whole, which is shorter than its diff:
```python
import functools

import jax
import jax.numpy as jnp
from jax import lax
from jax.experimental import pallas as pl
from jax.experimental.pallas import tpu as pltpu
from jax.sharding import PartitionSpec as P

K = 256
DS = 16
LANES = 128
PER = LANES // DS
MESH = pl.DeviceIdType.MESH
F32 = jnp.float32
BF16 = jnp.bfloat16


def one_hot(code_row, kinds):
    return jnp.where(code_row.astype(BF16) == kinds, 1.0, 0.0).astype(BF16)


def kernel(
    n_row, n_feat, inverse,
    v_ref, r_ref, codes_ref, cent_ref, grad_ref,
    code_in, codes_all, weights, kinds_ref,
    part, got_core, sum_core, got_feat, sum_feat, got_x, sum_x, got_z,
    table, table_t, recon,
    g_part, g_got_core, g_sum_core, g_got_x, g_sum_x, g_got_z,
    code_sems, s_core, s_feat, s_x, s_z, t_z, t_x, t_feat, t_core, g_core, g_x, g_z,
):
    rows, local = v_ref.shape
    groups = codes_ref.shape[0]
    deep = n_row // 4
    own = K // n_row
    tiles = local // LANES
    me_r, me_f = lax.axis_index("row"), lax.axis_index("feat")
    core, x, z = me_r % 2, (me_r // 2) % 2, me_r // 4

    def at(zz, xx, cc):
        return {"row": (zz * 2 + xx) * 2 + cc}

    sib_core, sib_x = at(z, x, 1 - core), at(z, 1 - x, core)
    z_peers = [at((z + s) % deep, x, core) for s in range(1, deep)]
    f_peers = [{"feat": (me_f + s) % n_feat} for s in range(1, n_feat)]

    barrier = pltpu.get_barrier_semaphore()
    everyone = [sib_core, sib_x] + z_peers + f_peers
    for peer in everyone:
        pl.semaphore_signal(barrier, inc=1, device_id=peer, device_id_type=MESH)
    pl.semaphore_wait(barrier, len(everyone))

    def remote(src, dst, sems, peer):
        return pltpu.make_async_remote_copy(
            src_ref=src, dst_ref=dst, send_sem=sems.at[0], recv_sem=sems.at[1],
            device_id=peer, device_id_type=MESH,
        )

    sends = [
        remote(codes_ref, code_in.at[s], code_sems.at[s], f_peers[s])
        for s in range(n_feat - 1)
    ]
    for copy in sends:
        copy.start()
    place = lax.broadcasted_iota(jnp.int32, (K, LANES), 0)
    chunk, inside = place // own, place % own
    pz, px, pc = chunk % deep, (chunk // deep) % 2, chunk // (2 * deep)
    kinds_ref[...] = (((pz * 2 + px) * 2 + pc) * own + inside).astype(F32).astype(BF16)
    codes_all[pl.ds(pl.multiple_of(me_f * groups, 8), groups), :] = codes_ref[...].astype(F32)
    for s in range(n_feat - 1):
        sends[s].wait()
        source = (me_f - (s + 1) + n_feat) % n_feat
        codes_all[pl.ds(pl.multiple_of(source * groups, 8), groups), :] = code_in[s].astype(F32)

    def hot_of(row):
        kinds = jnp.concatenate([kinds_ref[...]] * (rows // LANES), axis=1)
        return one_hot(codes_all[pl.ds(row, 1), :], kinds)

    lane = lax.broadcasted_iota(jnp.int32, (1, LANES), 1)

    def build(f, q):
        column = pl.multiple_of(f * local + q * LANES, LANES)
        rot = jnp.dot(v_ref[...], r_ref[:, pl.ds(column, LANES)], preferred_element_type=F32)
        high = rot.astype(BF16)
        low = pltpu.roll(rot - high.astype(F32), LANES // 2, 1)
        for side in range(2):
            weights[side, :, :LANES] = high
        weights[0, :, LANES:] = jnp.where(lane < LANES // 2, 1.0, low).astype(BF16)
        weights[1, :, LANES:] = jnp.where(lane < LANES // 2, low, 1.0).astype(BF16)

    def sum_tile(df, q):
        f = (me_f + df) % n_feat
        build(f, q)

        def one(i, carry):
            hot = hot_of(f * groups + q * PER + i)
            both = jnp.dot(hot, weights[i // (PER // 2)], preferred_element_type=F32)
            mine = lane // DS == i
            first, second = both[:, :LANES], both[:, LANES:]
            total = first + pltpu.roll(second, LANES // 2, 1)
            part[q, df] = jnp.where(mine, total, part[q, df])

            @pl.when(df == 0)
            def _():
                part[q, n_feat] = jnp.where(mine, second, part[q, n_feat])

            return carry

        lax.fori_loop(0, PER, one, 0)

    half, quarter = K // 2, K // 4

    def core_copy(q):
        return remote(
            part.at[q, :, pl.ds((1 - core) * half, half)], got_core.at[q], s_core.at[q], sib_core
        )

    def feat_copies(q):
        return [
            remote(sum_core.at[q, s], got_feat.at[q, s - 1], s_feat.at[q, s - 1], f_peers[s - 1])
            for s in range(1, n_feat)
        ]

    def x_copy(q):
        return remote(
            sum_feat.at[q, :, pl.ds((1 - x) * quarter, quarter)], got_x.at[q], s_x.at[q], sib_x
        )

    def z_copies(q):
        return [
            remote(
                sum_x.at[q, :, pl.ds(((z + s) % deep) * own, own)], got_z.at[q, s - 1],
                s_z.at[q, s - 1], z_peers[s - 1],
            )
            for s in range(1, deep)
        ]

    def stage(s, q):
        if s == 0:
            core_copy(q).start()
        elif s == 1:
            core_copy(q).wait()
            sum_core[q] = part[q, :, pl.ds(core * half, half)] + got_core[q]
            for copy in feat_copies(q):
                copy.start()
        elif s == 2:
            for copy in feat_copies(q):
                copy.wait()
            total = sum_core[q, 0]
            for i in range(n_feat - 1):
                total = total + got_feat[q, i]
            sum_feat[q, 0] = total
            sum_feat[q, 1] = sum_core[q, n_feat]
            x_copy(q).start()
        elif s == 3:
            x_copy(q).wait()
            sum_x[q] = sum_feat[q, :, pl.ds(x * quarter, quarter)] + got_x[q]
            for copy in z_copies(q):
                copy.start()
        else:
            for copy in z_copies(q):
                copy.wait()
            total = sum_x[q, :, pl.ds(z * own, own)]
            for i in range(deep - 1):
                total = total + got_z[q, i]
            mean = total[0] / (total[1] + 1.0)
            columns = pl.ds(pl.multiple_of(q * LANES, LANES), LANES)
            cent_ref[:, columns] = mean
            table[core, me_f, x, z, :, columns] = mean.astype(BF16)

    steps = tiles * n_feat

    def first_phase(t, carry):
        for s in range(5):
            g = t - n_feat - s

            @pl.when((g >= 0) & (g % n_feat == 0) & (g // n_feat < tiles))
            def _():
                stage(s, g // n_feat)

        @pl.when(t < steps)
        def _():
            sum_tile((n_feat - 1) - t % n_feat, t // n_feat)

        return carry

    lax.fori_loop(0, steps + 5, first_phase, 0)

    def gather(copies):
        for copy in copies:
            copy.start()
        for copy in copies:
            copy.wait()

    def same(piece, sems, peer):
        return remote(piece, piece, sems, peer)

    gather([
        same(table.at[core, me_f, x, z], t_z.at[s], z_peers[s]) for s in range(deep - 1)
    ])
    gather([same(table.at[core, me_f, x], t_x, sib_x)])
    gather([same(table.at[core, me_f], t_feat.at[s], f_peers[s]) for s in range(n_feat - 1)])
    gather([same(table.at[core], t_core, sib_core)])
    for f in range(n_feat):
        for q in range(tiles):
            block = table[:, f, :, :, :, q * LANES:(q + 1) * LANES].astype(F32).reshape(K, LANES)
            table_t[pl.ds(f * local + q * LANES, LANES), :] = block.T.astype(BF16)

    rounds = grad_ref.shape[0] // DS
    g_rows = n_row * DS
    g_half, g_quarter = g_rows // 2, g_rows // 4

    def g_core_copy(j):
        return remote(
            g_part.at[j, pl.ds((1 - core) * g_half, g_half)], g_got_core.at[j], g_core.at[j], sib_core
        )

    def g_x_copy(j):
        return remote(
            g_sum_core.at[j, pl.ds((1 - x) * g_quarter, g_quarter)], g_got_x.at[j], g_x.at[j], sib_x
        )

    def g_z_copies(j):
        return [
            remote(
                g_sum_x.at[j, pl.ds(((z + s) % deep) * DS, DS)], g_got_z.at[j, s - 1],
                g_z.at[j, s - 1], z_peers[s - 1],
            )
            for s in range(1, deep)
        ]

    def g_stage(s, j):
        if s == 0:
            g_core_copy(j).start()
        elif s == 1:
            g_core_copy(j).wait()
            g_sum_core[j] = g_part[j, pl.ds(core * g_half, g_half)] + g_got_core[j]
            g_x_copy(j).start()
        elif s == 2:
            g_x_copy(j).wait()
            g_sum_x[j] = g_sum_core[j, pl.ds(x * g_quarter, g_quarter)] + g_got_x[j]
            for copy in g_z_copies(j):
                copy.start()
        else:
            for copy in g_z_copies(j):
                copy.wait()
            total = g_sum_x[j, pl.ds(z * DS, DS)]
            for i in range(deep - 1):
                total = total + g_got_z[j, i]
            grad_ref[pl.ds(pl.multiple_of(j * DS, DS), DS), :] = total

    def rebuild(j, lo, count):
        def one(i, carry):
            p = lo + i
            pz, px, pc = p % deep, (p // deep) % 2, p // (2 * deep)
            m = ((pz * 2 + px) * 2 + pc) * rounds + j
            part_t = table_t[pl.ds(pl.multiple_of(m * DS, DS), DS), :]
            made = jnp.dot(part_t, hot_of(m), preferred_element_type=F32)
            recon[pl.ds(pl.multiple_of(p * DS, DS), DS), :] = made.astype(BF16)
            return carry

        lax.fori_loop(0, count, one, 0)

    def second_phase(t, carry):
        for s in range(4):
            g = t - 2 - s

            @pl.when((g >= 0) & (g % 2 == 0) & (g // 2 < rounds))
            def _():
                g_stage(s, g // 2)

        @pl.when(t < 2 * rounds)
        def _():
            j = t // 2
            rebuild(j, (t % 2) * (n_row // 2), n_row // 2)

            @pl.when(t % 2 == 1)
            def _():
                g_part[j] = inverse * jnp.dot(
                    recon[...], v_ref[...], preferred_element_type=F32
                )

        return carry

    lax.fori_loop(0, 2 * rounds + 4, second_phase, 0)


def shards(vectors, rotation, codes, live_rows):
    rows, local = vectors.shape
    groups = codes.shape[1]
    n_row, n_feat = lax.axis_size("row"), lax.axis_size("feat")
    deep, own, tiles = n_row // 4, K // n_row, local // LANES
    out_rows = n_feat * local // n_row
    rounds, g_rows = out_rows // DS, n_row * DS
    keep = jnp.arange(rows, dtype=jnp.int32) < live_rows[0]
    coded = jnp.where(keep[:, None], codes, -1).astype(BF16).T
    vmem = pltpu.VMEM
    sem = pltpu.SemaphoreType.DMA
    return pl.pallas_call(
        functools.partial(kernel, n_row, n_feat, 1.0 / (rows * n_row)),
        out_shape=(
            jax.ShapeDtypeStruct((own, local), F32),
            jax.ShapeDtypeStruct((out_rows, local), F32),
        ),
        in_specs=[pl.BlockSpec(memory_space=vmem)] * 3,
        out_specs=(pl.BlockSpec(memory_space=vmem),) * 2,
        scratch_shapes=[
            vmem((max(n_feat - 1, 1), groups, rows), BF16),
            vmem((n_feat * groups, rows), F32),
            vmem((2, rows, 2 * LANES), BF16),
            vmem((K, LANES), BF16),
            vmem((tiles, n_feat + 1, K, LANES), F32),
            vmem((tiles, n_feat + 1, K // 2, LANES), F32),
            vmem((tiles, n_feat + 1, K // 2, LANES), F32),
            vmem((tiles, max(n_feat - 1, 1), K // 2, LANES), F32),
            vmem((tiles, 2, K // 2, LANES), F32),
            vmem((tiles, 2, K // 4, LANES), F32),
            vmem((tiles, 2, K // 4, LANES), F32),
            vmem((tiles, max(deep - 1, 1), 2, own, LANES), F32),
            vmem((2, n_feat, 2, deep, own, local), BF16),
            vmem((n_feat * local, K), BF16),
            vmem((g_rows, rows), BF16),
            vmem((rounds, g_rows, local), F32),
            vmem((rounds, g_rows // 2, local), F32),
            vmem((rounds, g_rows // 2, local), F32),
            vmem((rounds, g_rows // 4, local), F32),
            vmem((rounds, g_rows // 4, local), F32),
            vmem((rounds, max(deep - 1, 1), DS, local), F32),
            sem((max(n_feat - 1, 1), 2)),
            sem((tiles, 2)),
            sem((tiles, max(n_feat - 1, 1), 2)),
            sem((tiles, 2)),
            sem((tiles, max(deep - 1, 1), 2)),
            sem((max(deep - 1, 1), 2)),
            sem((2,)),
            sem((max(n_feat - 1, 1), 2)),
            sem((2,)),
            sem((rounds, 2)),
            sem((rounds, 2)),
            sem((rounds, max(deep - 1, 1), 2)),
        ],
        compiler_params=pltpu.CompilerParams(
            collective_id=0, has_side_effects=True, vmem_limit_bytes=56 * 1024 * 1024
        ),
    )(vectors, rotation, coded)


def solution(mesh):
    return jax.shard_map(
        shards,
        mesh=mesh,
        in_specs=(P("row", "feat"), P("feat", None), P("row", "feat"), P("row")),
        out_specs=(P("row", "feat"), P("row", "feat")),
        check_vma=False,
    )
```

time: 367 us -> 143 us (0.39)
  waiting for transfers between devices: 213 us -> 0 us
  Pallas kernels: 0 us -> 137 us
  matrix products: 58.9 us -> 0 us
  other arithmetic: 41.4 us -> 1.68 us
  blocking collectives: 20.1 us -> 0 us
  between operations: 16.4 us -> 1.29 us
  local copies, waits for them, and re-layouts: 11.6 us -> 2.94 us
  starting transfers between devices: 4.4 us -> 0 us
    pallas_call x0 -> x1, Pallas kernels: none -> 137 us  [shards(): pl.pallas_call(functools.partial(kernel, n_row, n_feat, 1.0 / (rows * n_r...]
    reduce_scatter x3 -> x0, waiting for transfers between devices: 117 us -> none  [the longest x1 61.6 us: shards(): lax.psum_scatter(product * inverse, 'row', scatter_dimension=0, tiled=True)]
    all_gather x2 -> x0, waiting for transfers between devices: 95.4 us -> none  [the longest x1 65.9 us: shards(): recon = lax.all_gather(local_recon, 'feat', axis=1, tiled=True)]
    dot_general x8 -> x0, matrix products: 58.9 us -> none  [the longest x5 29 us: add_block(): jnp.einsum('nmk,nmd->kmd', hot_block, rot_block, precision=lax.Precision....]
    reduce_sum x1 -> x0, other arithmetic: 21.3 us -> none  [shards(): counts = jnp.sum(hot, axis=0, dtype=jnp.float32).T]
    all_gather x1 -> x0, blocking collectives: 20.1 us -> none  [shards(): lax.all_gather(centroids.astype(jnp.bfloat16), 'row', axis=0, tiled=True)]
    mul x1 -> x0, other arithmetic: 18 us -> none  [make_hot(): (code_block[:, :, None] == kinds[None, None, :]).astype(jnp.bfloat16)]
    dynamic_slice x5 -> x0, local copies, waits for them, and re-layouts: 6.54 us -> none  [add_block(): lax.dynamic_slice_in_dim(rotated, index * step_rows, step_rows, 0)]
  transfers between devices with their start and end apart: 6 -> 0, of which waited for: 4 -> 0; matrix products, arithmetic and copies ran while one was open for 24% -> 0% of each run, Pallas kernels for 0% -> 0%
where the time goes in v1:
time: 143 us
  Pallas kernels  137 us (96%)
  local copies, waits for them, and re-layouts  2.94 us (2%)
  other arithmetic  1.68 us (1%)
    pallas_call x1, Pallas kernels, shards(): pl.pallas_call(functools.partial(kernel, n_row, n_feat, 1.0 / (rows * n_r...  137 us
    unnamed x2, local copies, waits for them, and re-layouts  2.94 us

profile of v1, /device:TPU:0, one launch (start us, length us, event | category | flops | bytes accessed | tf_op | source)
XLA Modules:
  0.0 143.2 jit_solution(17922612323226020609)
XLA Ops:
  1.3 1.7 %fusion.codes_ref = bf16[32,2560]{1,0:T(8,128)(2,1)} fusion(s32[2560,32]{0,1:T(8,128)} %param.6, pred[2560]{0:T(1024)(128)(4,1)S(1)} %iota_compare_fusion), kind=kLoop, calls=%fused_computation.1 | loop fusion | flops 163840 | bytes 494080 | tf_op jit(solution)/shard_map/transpose | solution.py:296
  3.0 137.3 %shard_map.59 = (f32[16,512]{1,0:T(8,128)}, f32[64,512]{1,0:T(8,128)}) custom-call(bf16[2560,512]{1,0:T(8,128)(2,1)} %v_ref.1, bf16[512,1024]{1,0:T(8,128)(2,1)} %r_ref.1, bf16[32,2560]{1,0:T(8,128)(2,1)} %fusion.codes_ref), custom_call_target="tpu_custom_call" | custom-call | tf_op jit(solution)/shard_map/pallas_call | solution.py:299
  140.3 1.4 copy.9
  141.7 1.6 %copy.10 = f32[64,512]{1,0:T(8,128)} copy(f32[64,512]{1,0:T(8,128)} %get-tuple-element.5) | data formatting | bytes 262144
  (1 shorter events, 0.0 us)

commit v2 on v1

--- a/solution.py
+++ b/solution.py
@@ -17,13 +17,13 @@
 
 
 def one_hot(code_row, kinds):
-    return jnp.where(code_row.astype(BF16) == kinds, 1.0, 0.0).astype(BF16)
+    return jnp.where(code_row.astype(BF16) == kinds, jnp.ones((), BF16), jnp.zeros((), BF16))
 
 
 def kernel(
     n_row, n_feat, inverse,
     v_ref, r_ref, codes_ref, cent_ref, grad_ref,
-    code_in, codes_all, weights, kinds_ref,
+    code_in, codes_all, weights, sums_t, counts_t, kinds_ref,
     part, got_core, sum_core, got_feat, sum_feat, got_x, sum_x, got_z,
     table, table_t, recon,
     g_part, g_got_core, g_sum_core, g_got_x, g_sum_x, g_got_z,
@@ -76,17 +76,18 @@
         kinds = jnp.concatenate([kinds_ref[...]] * (rows // LANES), axis=1)
         return one_hot(codes_all[pl.ds(row, 1), :], kinds)
 
-    lane = lax.broadcasted_iota(jnp.int32, (1, LANES), 1)
+    nt = (((1,), (1,)), ((), ()))
+    weights[:, 2 * DS:, :] = jnp.ones((PER, DS, rows), BF16)
 
     def build(f, q):
         column = pl.multiple_of(f * local + q * LANES, LANES)
-        rot = jnp.dot(v_ref[...], r_ref[:, pl.ds(column, LANES)], preferred_element_type=F32)
+        turned = r_ref[:, pl.ds(column, LANES)].astype(F32).T.astype(BF16)
+        rot = lax.dot_general(turned, v_ref[...], nt, preferred_element_type=F32)
         high = rot.astype(BF16)
-        low = pltpu.roll(rot - high.astype(F32), LANES // 2, 1)
-        for side in range(2):
-            weights[side, :, :LANES] = high
-        weights[0, :, LANES:] = jnp.where(lane < LANES // 2, 1.0, low).astype(BF16)
-        weights[1, :, LANES:] = jnp.where(lane < LANES // 2, low, 1.0).astype(BF16)
+        low = (rot - high.astype(F32)).astype(BF16)
+        for i in range(PER):
+            weights[i, :DS] = high[i * DS:(i + 1) * DS]
+            weights[i, DS:2 * DS] = low[i * DS:(i + 1) * DS]
 
     def sum_tile(df, q):
         f = (me_f + df) % n_feat
@@ -94,19 +95,18 @@
 
         def one(i, carry):
             hot = hot_of(f * groups + q * PER + i)
-            both = jnp.dot(hot, weights[i // (PER // 2)], preferred_element_type=F32)
-            mine = lane // DS == i
-            first, second = both[:, :LANES], both[:, LANES:]
-            total = first + pltpu.roll(second, LANES // 2, 1)
-            part[q, df] = jnp.where(mine, total, part[q, df])
-
-            @pl.when(df == 0)
-            def _():
-                part[q, n_feat] = jnp.where(mine, second, part[q, n_feat])
-
+            both = lax.dot_general(weights[i], hot, nt, preferred_element_type=F32)
+            features = pl.ds(pl.multiple_of(i * DS, DS), DS)
+            sums_t[features, :] = both[:DS] + both[DS:2 * DS]
+            counts_t[features, :] = both[2 * DS:]
             return carry
 
         lax.fori_loop(0, PER, one, 0)
+        part[q, df] = sums_t[...].T
+
+        @pl.when(df == 0)
+        def _():
+            part[q, n_feat] = counts_t[...].T
 
     half, quarter = K // 2, K // 4
 
@@ -307,7 +307,9 @@
         scratch_shapes=[
             vmem((max(n_feat - 1, 1), groups, rows), BF16),
             vmem((n_feat * groups, rows), F32),
-            vmem((2, rows, 2 * LANES), BF16),
+            vmem((PER, 3 * DS, rows), BF16),
+            vmem((LANES, K), F32),
+            vmem((LANES, K), F32),
             vmem((K, LANES), BF16),
             vmem((tiles, n_feat + 1, K, LANES), F32),
             vmem((tiles, n_feat + 1, K // 2, LANES), F32),

time: 143 us -> 125 us (0.87)
  Pallas kernels: 137 us -> 119 us
    pallas_call x1, Pallas kernels: 137 us -> 119 us  [shards(): pl.pallas_call(functools.partial(kernel, n_row, n_feat, 1.0 / (rows * n_r...]
where the time goes in v2:
time: 125 us
  Pallas kernels  119 us (95%)
  local copies, waits for them, and re-layouts  2.94 us (2%)
  other arithmetic  1.68 us (1%)
  between operations  1.29 us (1%)
    pallas_call x1, Pallas kernels, shards(): pl.pallas_call(functools.partial(kernel, n_row, n_feat, 1.0 / (rows * n_r...  119 us
    unnamed x2, local copies, waits for them, and re-layouts  2.94 us

profile of v2, /device:TPU:0, one launch (start us, length us, event | category | flops | bytes accessed | tf_op | source)
XLA Modules:
  0.0 125.2 jit_solution(6575657579217594186)
XLA Ops:
  1.3 1.7 %fusion.codes_ref = bf16[32,2560]{1,0:T(8,128)(2,1)} fusion(s32[2560,32]{0,1:T(8,128)} %param.6, pred[2560]{0:T(1024)(128)(4,1)S(1)} %iota_compare_fusion), kind=kLoop, calls=%fused_computation.1 | loop fusion | flops 163840 | bytes 494080 | tf_op jit(solution)/shard_map/transpose | solution.py:296
  3.0 119.3 %shard_map.59 = (f32[16,512]{1,0:T(8,128)}, f32[64,512]{1,0:T(8,128)}) custom-call(bf16[2560,512]{1,0:T(8,128)(2,1)} %v_ref.1, bf16[512,1024]{1,0:T(8,128)(2,1)} %r_ref.1, bf16[32,2560]{1,0:T(8,128)(2,1)} %fusion.codes_ref), custom_call_target="tpu_custom_call" | custom-call | tf_op jit(solution)/shard_map/pallas_call | solution.py:299
  122.3 1.4 %copy.9 = f32[16,512]{1,0:T(8,128)} copy(f32[16,512]{1,0:T(8,128)} %get-tuple-element.4) | data formatting | bytes 65536
  123.7 1.6 %copy.10 = f32[64,512]{1,0:T(8,128)} copy(f32[64,512]{1,0:T(8,128)} %get-tuple-element.5) | data formatting | bytes 262144
  (1 shorter events, 0.0 us)

commit v3 on v2

v3 whole, which is shorter than its diff:
```python
import functools

import jax
import jax.numpy as jnp
from jax import lax
from jax.experimental import pallas as pl
from jax.experimental.pallas import tpu as pltpu
from jax.sharding import PartitionSpec as P

K = 256
DS = 16
LANES = 128
PER = LANES // DS
MESH = pl.DeviceIdType.MESH
F32 = jnp.float32
BF16 = jnp.bfloat16


def one_hot(code_row, kinds):
    return jnp.where(code_row.astype(BF16) == kinds, jnp.ones((), BF16), jnp.zeros((), BF16))


def kernel(
    n_row, n_feat, inverse,
    v_ref, r_ref, codes_ref, cent_ref, grad_ref,
    code_in, codes_all, kinds_ref, r_tiles, hots, gathered,
    part, got_core, sum_core, got_feat, sum_feat, got_x, sum_x, got_z,
    table, table_t,
    g_part, g_got_core, g_sum_core, g_got_x, g_sum_x, g_got_z,
    code_sems, s_core, s_feat, s_x, s_z, t_z, t_x, t_feat, t_core, g_core, g_x, g_z,
):
    rows, local = v_ref.shape
    groups = codes_ref.shape[0]
    deep = n_row // 4
    own = K // n_row
    tiles = local // LANES
    per = PER * n_feat // n_row
    owned = tiles * per
    batch = PER // 2
    me_r, me_f = lax.axis_index("row"), lax.axis_index("feat")
    core, x, z = me_r % 2, (me_r // 2) % 2, me_r // 4

    def at(zz, xx, cc):
        return {"row": (zz * 2 + xx) * 2 + cc}

    sib_core, sib_x = at(z, x, 1 - core), at(z, 1 - x, core)
    z_peers = [at((z + s) % deep, x, core) for s in range(1, deep)]
    f_peers = [{"feat": (me_f + s) % n_feat} for s in range(1, n_feat)]

    barrier = pltpu.get_barrier_semaphore()
    everyone = [sib_core, sib_x] + z_peers + f_peers
    for peer in everyone:
        pl.semaphore_signal(barrier, inc=1, device_id=peer, device_id_type=MESH)
    pl.semaphore_wait(barrier, len(everyone))

    def remote(src, dst, sems, peer):
        return pltpu.make_async_remote_copy(
            src_ref=src, dst_ref=dst, send_sem=sems.at[0], recv_sem=sems.at[1],
            device_id=peer, device_id_type=MESH,
        )

    sends = [
        remote(codes_ref, code_in.at[s], code_sems.at[s], f_peers[s])
        for s in range(n_feat - 1)
    ]
    for copy in sends:
        copy.start()
    place = lax.broadcasted_iota(jnp.int32, (K, LANES), 0)
    chunk, inside = place // own, place % own
    pz, px, pc = chunk % deep, (chunk // deep) % 2, chunk // (2 * deep)
    kinds_ref[...] = (((pz * 2 + px) * 2 + pc) * own + inside).astype(F32).astype(BF16)
    codes_all[pl.ds(pl.multiple_of(me_f * groups, 8), groups), :] = codes_ref[...].astype(F32)

    def member(i, q):
        return (i // per) * owned + q * per + i % per

    for f in range(n_feat):
        block = r_ref[:, f * local:(f + 1) * local].astype(F32)
        for q in range(tiles):
            r_tiles[f * tiles + q] = jnp.concatenate(
                [block[:, member(i, q) * DS:(member(i, q) + 1) * DS] for i in range(PER)], axis=1
            ).astype(BF16)
    for s in range(n_feat - 1):
        sends[s].wait()
        source = (me_f - (s + 1) + n_feat) % n_feat
        codes_all[pl.ds(pl.multiple_of(source * groups, 8), groups), :] = code_in[s].astype(F32)

    lane = lax.broadcasted_iota(jnp.int32, (1, LANES), 1)

    def sum_half(df, q, h):
        f = (me_f + df) % n_feat
        kinds = jnp.concatenate([kinds_ref[...]] * (rows // LANES), axis=1)
        ids = [f * groups + member(h * batch + i, q) for i in range(batch)]
        for i in range(batch):
            hots[i * K:(i + 1) * K, :] = one_hot(codes_all[pl.ds(ids[i], 1), :], kinds)
        full = jnp.dot(hots[...], v_ref[...], preferred_element_type=F32)
        high = full.astype(BF16)
        low = (full - high.astype(F32)).astype(BF16)
        r_tile = r_tiles[f * tiles + q]
        sums = jnp.dot(high, r_tile, preferred_element_type=F32) + jnp.dot(
            low, r_tile, preferred_element_type=F32
        )
        for i in range(batch):
            gathered[ids[i], :K] = high[i * K:(i + 1) * K]
            gathered[ids[i], K:] = low[i * K:(i + 1) * K]
            mine = lane // DS == h * batch + i
            part[q, df] = jnp.where(mine, sums[i * K:(i + 1) * K], part[q, df])

        @pl.when(df == 0)
        def _():
            ones = jnp.ones((LANES, LANES), BF16)
            for i in range(batch):
                some = hots[i * K:(i + 1) * K, :LANES]
                for c in range(1, rows // LANES):
                    some = some + hots[i * K:(i + 1) * K, c * LANES:(c + 1) * LANES]
                count = jnp.dot(some, ones, preferred_element_type=F32)
                mine = lane // DS == h * batch + i
                part[q, n_feat] = jnp.where(mine, count, part[q, n_feat])

    half, quarter = K // 2, K // 4

    def core_copy(q):
        return remote(
            part.at[q, :, pl.ds((1 - core) * half, half)], got_core.at[q], s_core.at[q], sib_core
        )

    def feat_copies(q):
        return [
            remote(sum_core.at[q, s], got_feat.at[q, s - 1], s_feat.at[q, s - 1], f_peers[s - 1])
            for s in range(1, n_feat)
        ]

    def x_copy(q):
        return remote(
            sum_feat.at[q, :, pl.ds((1 - x) * quarter, quarter)], got_x.at[q], s_x.at[q], sib_x
        )

    def z_copies(q):
        return [
            remote(
                sum_x.at[q, :, pl.ds(((z + s) % deep) * own, own)], got_z.at[q, s - 1],
                s_z.at[q, s - 1], z_peers[s - 1],
            )
            for s in range(1, deep)
        ]

    def same(piece, sems, peer):
        return remote(piece, piece, sems, peer)

    def table_z(q):
        piece = table.at[q, core, me_f, x, z]
        return [same(piece, t_z.at[q, s], z_peers[s]) for s in range(deep - 1)]

    def table_x(q):
        return [same(table.at[q, core, me_f, x], t_x.at[q], sib_x)]

    def table_feat(q):
        piece = table.at[q, core, me_f]
        return [same(piece, t_feat.at[q, s], f_peers[s]) for s in range(n_feat - 1)]

    def table_core(q):
        return [same(table.at[q, core], t_core.at[q], sib_core)]

    deal = per * DS
    g_half, g_quarter = n_row * deal // 2, n_row * deal // 4

    def g_core_copy(q):
        return remote(
            g_part.at[q, pl.ds((1 - core) * g_half, g_half)], g_got_core.at[q], g_core.at[q], sib_core
        )

    def g_x_copy(q):
        return remote(
            g_sum_core.at[q, pl.ds((1 - x) * g_quarter, g_quarter)], g_got_x.at[q], g_x.at[q], sib_x
        )

    def g_z_copies(q):
        return [
            remote(
                g_sum_x.at[q, pl.ds(((z + s) % deep) * deal, deal)], g_got_z.at[q, s - 1],
                g_z.at[q, s - 1], z_peers[s - 1],
            )
            for s in range(1, deep)
        ]

    def gradient(q):
        def one(i, carry):
            p, e = i // per, i % per
            gz, gx, gc = p % deep, (p // deep) % 2, p // (2 * deep)
            r = (gz * 2 + gx) * 2 + gc
            line = table_t[q, pl.ds(pl.multiple_of((r * per + e) * DS, DS), DS), :]
            made = jnp.dot(line, gathered[r * owned + q * per + e], preferred_element_type=F32)
            g_part[q, pl.ds(pl.multiple_of(i * DS, DS), DS), :] = made * inverse
            return carry

        lax.fori_loop(0, n_row * per, one, 0)

    def start(copies):
        for copy in copies:
            copy.start()

    def wait(copies):
        for copy in copies:
            copy.wait()

    def stage(s, q):
        if s == 0:
            core_copy(q).start()
        elif s == 1:
            core_copy(q).wait()
            sum_core[q] = part[q, :, pl.ds(core * half, half)] + got_core[q]
            start(feat_copies(q))
        elif s == 2:
            wait(feat_copies(q))
            total = sum_core[q, 0]
            for i in range(n_feat - 1):
                total = total + got_feat[q, i]
            sum_feat[q, 0] = total
            sum_feat[q, 1] = sum_core[q, n_feat]
            x_copy(q).start()
        elif s == 3:
            x_copy(q).wait()
            sum_x[q] = sum_feat[q, :, pl.ds(x * quarter, quarter)] + got_x[q]
            start(z_copies(q))
        elif s == 4:
            wait(z_copies(q))
            total = sum_x[q, :, pl.ds(z * own, own)]
            for i in range(deep - 1):
                total = total + got_z[q, i]
            mean = total[0] / (total[1] + 1.0)
            cent_ref[q] = mean
            table[q, core, me_f, x, z] = mean.astype(BF16)
            start(table_z(q))
        elif s == 5:
            wait(table_z(q))
            start(table_x(q))
        elif s == 6:
            wait(table_x(q))
            start(table_feat(q))
        elif s == 7:
            wait(table_feat(q))
            start(table_core(q))
        elif s == 8:
            wait(table_core(q))
            for f in range(n_feat):
                turned = table[q, :, f].astype(F32).reshape(K, LANES).T.astype(BF16)
                for side in range(2):
                    table_t[q, f * LANES:(f + 1) * LANES, side * K:(side + 1) * K] = turned
            gradient(q)
            g_core_copy(q).start()
        elif s == 9:
            g_core_copy(q).wait()
            g_sum_core[q] = g_part[q, pl.ds(core * g_half, g_half)] + g_got_core[q]
            g_x_copy(q).start()
        elif s == 10:
            g_x_copy(q).wait()
            g_sum_x[q] = g_sum_core[q, pl.ds(x * g_quarter, g_quarter)] + g_got_x[q]
            start(g_z_copies(q))
        else:
            wait(g_z_copies(q))
            total = g_sum_x[q, pl.ds(z * deal, deal)]
            for i in range(deep - 1):
                total = total + g_got_z[q, i]
            grad_ref[pl.ds(pl.multiple_of(q * deal, deal), deal), :] = total

    stages = 12
    each = 2 * n_feat
    steps = tiles * each

    def step(t, carry):
        for s in reversed(range(stages)):
            g = t - each - s

            @pl.when((g >= 0) & (g % each == 0) & (g // each < tiles))
            def _():
                stage(s, g // each)

        @pl.when(t < steps)
        def _():
            sum_half((n_feat - 1) - (t % each) // 2, t // each, t % 2)

        return carry

    lax.fori_loop(0, steps + stages, step, 0)


def shards(vectors, rotation, codes, live_rows):
    rows, local = vectors.shape
    groups = codes.shape[1]
    n_row, n_feat = lax.axis_size("row"), lax.axis_size("feat")
    deep, own, tiles = n_row // 4, K // n_row, local // LANES
    out_rows = n_feat * local // n_row
    per = PER * n_feat // n_row
    deal = per * DS
    g_rows = n_row * deal
    others, far = max(n_feat - 1, 1), max(deep - 1, 1)
    keep = jnp.arange(rows, dtype=jnp.int32) < live_rows[0]
    coded = jnp.where(keep[:, None], codes, -1).astype(BF16).T
    vmem = pltpu.VMEM
    sem = pltpu.SemaphoreType.DMA
    means, grad_t = pl.pallas_call(
        functools.partial(kernel, n_row, n_feat, 1.0 / (rows * n_row)),
        out_shape=(
            jax.ShapeDtypeStruct((tiles, own, LANES), F32),
            jax.ShapeDtypeStruct((out_rows, local), F32),
        ),
        in_specs=[pl.BlockSpec(memory_space=vmem)] * 3,
        out_specs=(pl.BlockSpec(memory_space=vmem),) * 2,
        scratch_shapes=[
            vmem((others, groups, rows), BF16),
            vmem((n_feat * groups, rows), F32),
            vmem((K, LANES), BF16),
            vmem((n_feat * tiles, local, LANES), BF16),
            vmem((PER // 2 * K, rows), BF16),
            vmem((n_feat * groups, 2 * K, local), BF16),
            vmem((tiles, n_feat + 1, K, LANES), F32),
            vmem((tiles, n_feat + 1, K // 2, LANES), F32),
            vmem((tiles, n_feat + 1, K // 2, LANES), F32),
            vmem((tiles, others, K // 2, LANES), F32),
            vmem((tiles, 2, K // 2, LANES), F32),
            vmem((tiles, 2, K // 4, LANES), F32),
            vmem((tiles, 2, K // 4, LANES), F32),
            vmem((tiles, far, 2, own, LANES), F32),
            vmem((tiles, 2, n_feat, 2, deep, own, LANES), BF16),
            vmem((tiles, n_feat * LANES, 2 * K), BF16),
            vmem((tiles, g_rows, local), F32),
            vmem((tiles, g_rows // 2, local), F32),
            vmem((tiles, g_rows // 2, local), F32),
            vmem((tiles, g_rows // 4, local), F32),
            vmem((tiles, g_rows // 4, local), F32),
            vmem((tiles, far, deal, local), F32),
            sem((others, 2)),
            sem((tiles, 2)),
            sem((tiles, others, 2)),
            sem((tiles, 2)),
            sem((tiles, far, 2)),
            sem((tiles, far, 2)),
            sem((tiles, 2)),
            sem((tiles, others, 2)),
            sem((tiles, 2)),
            sem((tiles, 2)),
            sem((tiles, 2)),
            sem((tiles, far, 2)),
        ],
        compiler_params=pltpu.CompilerParams(
            collective_id=0, has_side_effects=True, vmem_limit_bytes=63 * 1024 * 1024
        ),
    )(vectors, rotation, coded)
    split = means.reshape(tiles, own, PER // per, per, DS)
    return split.transpose(1, 2, 0, 3, 4).reshape(own, local), grad_t


def solution(mesh):
    return jax.shard_map(
        shards,
        mesh=mesh,
        in_specs=(P("row", "feat"), P("feat", None), P("row", "feat"), P("row")),
        out_specs=(P("row", "feat"), P("row", "feat")),
        check_vma=False,
    )
```

time: 125 us -> 141 us (1.13)
  Pallas kernels: 119 us -> 134 us
    pallas_call x1, Pallas kernels: 119 us -> 134 us  [shards(): pl.pallas_call(functools.partial(kernel, n_row, n_feat, 1.0 / (rows * n_r...]
    reshape x0 -> x2, local copies, waits for them, and re-layouts: none -> 1.74 us  [the longest x1 0.88 us: shards(): split = means.reshape(tiles, own, PER // per, per, DS)]
    unnamed x2 -> x1, local copies, waits for them, and re-layouts: 2.94 us -> 1.57 us
where the time goes in v3:
time: 141 us
  Pallas kernels  134 us (95%)
  local copies, waits for them, and re-layouts  3.48 us (2%)
  other arithmetic  1.68 us (1%)
    pallas_call x1, Pallas kernels, shards(): pl.pallas_call(functools.partial(kernel, n_row, n_feat, 1.0 / (rows * n_r...  134 us

profile of v3, /device:TPU:0, one launch (start us, length us, event | category | flops | bytes accessed | tf_op | source)
XLA Modules:
  0.0 140.7 jit_solution(15396498094974132491)
XLA Ops:
  1.3 1.7 %fusion.codes_ref = bf16[32,2560]{1,0:T(8,128)(2,1)} fusion(s32[2560,32]{0,1:T(8,128)} %param.6, pred[2560]{0:T(1024)(128)(4,1)S(1)} %iota_compare_fusion), kind=kLoop, calls=%fused_computation.1 | loop fusion | flops 163840 | bytes 494080 | tf_op jit(solution)/shard_map/transpose | solution.py:298
  3.0 134.2 %shard_map.59 = (f32[4,16,128]{2,1,0:T(8,128)}, f32[64,512]{1,0:T(8,128)}) custom-call(bf16[2560,512]{1,0:T(8,128)(2,1)} %v_ref.1, bf16[512,1024]{1,0:T(8,128)(2,1)} %r_ref.1, bf16[32,2560]{1,0:T(8,128)(2,1)} %fusion.codes_ref), custom_call_target="tpu_custom_call" | custom-call | tf_op jit(solution)/shard_map/pallas_call | solution.py:301
  137.2 0.9 reshape.14
  138.1 0.2 copy.6
  138.2 0.9 reshape.15
  139.1 1.6 %copy.9 = f32[64,512]{1,0:T(8,128)} copy(f32[64,512]{1,0:T(8,128)} %get-tuple-element.9) | data formatting | bytes 262144
  (1 shorter events, 0.0 us)

commit v4 on v3

--- a/solution.py
+++ b/solution.py
@@ -23,9 +23,9 @@
 def kernel(
     n_row, n_feat, inverse,
     v_ref, r_ref, codes_ref, cent_ref, grad_ref,
-    code_in, codes_all, kinds_ref, r_tiles, hots, gathered,
+    code_in, codes_all, kinds_ref, r_tiles, weights, sums_t, counts_t,
     part, got_core, sum_core, got_feat, sum_feat, got_x, sum_x, got_z,
-    table, table_t,
+    table, table_t, recon,
     g_part, g_got_core, g_sum_core, g_got_x, g_sum_x, g_got_z,
     code_sems, s_core, s_feat, s_x, s_z, t_z, t_x, t_feat, t_core, g_core, g_x, g_z,
 ):
@@ -36,7 +36,7 @@
     tiles = local // LANES
     per = PER * n_feat // n_row
     owned = tiles * per
-    batch = PER // 2
+    half, quarter = K // 2, K // 4
     me_r, me_f = lax.axis_index("row"), lax.axis_index("feat")
     core, x, z = me_r % 2, (me_r // 2) % 2, me_r // 4
 
@@ -65,10 +65,8 @@
     ]
     for copy in sends:
         copy.start()
-    place = lax.broadcasted_iota(jnp.int32, (K, LANES), 0)
-    chunk, inside = place // own, place % own
-    pz, px, pc = chunk % deep, (chunk // deep) % 2, chunk // (2 * deep)
-    kinds_ref[...] = (((pz * 2 + px) * 2 + pc) * own + inside).astype(F32).astype(BF16)
+    kinds_ref[...] = lax.broadcasted_iota(jnp.int32, (half, LANES), 0).astype(F32).astype(BF16)
+    weights[:, 2 * DS:, :] = jnp.ones((n_feat * PER, DS, rows), BF16)
     codes_all[pl.ds(pl.multiple_of(me_f * groups, 8), groups), :] = codes_ref[...].astype(F32)
 
     def member(i, q):
@@ -77,47 +75,70 @@
     for f in range(n_feat):
         block = r_ref[:, f * local:(f + 1) * local].astype(F32)
         for q in range(tiles):
-            r_tiles[f * tiles + q] = jnp.concatenate(
+            r_tiles[q, f * LANES:(f + 1) * LANES] = jnp.concatenate(
                 [block[:, member(i, q) * DS:(member(i, q) + 1) * DS] for i in range(PER)], axis=1
-            ).astype(BF16)
+            ).T.astype(BF16)
     for s in range(n_feat - 1):
         sends[s].wait()
         source = (me_f - (s + 1) + n_feat) % n_feat
         codes_all[pl.ds(pl.multiple_of(source * groups, 8), groups), :] = code_in[s].astype(F32)
 
-    lane = lax.broadcasted_iota(jnp.int32, (1, LANES), 1)
+    nt = (((1,), (1,)), ((), ()))
+
+    def pair(first, second):
+        kinds = jnp.concatenate([kinds_ref[...]] * (rows // LANES), axis=1)
+        hots, uppers = [], []
+        for m in (first, second):
+            row = codes_all[pl.ds(m, 1), :]
+            upper = row >= half
+            hots.append(one_hot(jnp.where(upper, row - half, row), kinds))
+            uppers.append(upper)
+        return jnp.concatenate(hots, axis=0), uppers
+
+    def build(q):
+        rot = lax.dot_general(r_tiles[q], v_ref[...], nt, preferred_element_type=F32)
+        high = rot.astype(BF16)
+        low = (rot - high.astype(F32)).astype(BF16)
+        for i in range(n_feat * PER):
+            weights[i, :DS] = high[i * DS:(i + 1) * DS]
+            weights[i, DS:2 * DS] = low[i * DS:(i + 1) * DS]
+
+    def sum_pair(f, q, i):
+        ids = [f * groups + member(i + n, q) for n in range(2)]
+        hots, uppers = pair(*ids)
+        lines = []
+        for n in range(2):
+            line = weights[f * PER + i + n]
+            up = jnp.where(uppers[n], 1.0, 0.0)
+            lines += [line * (1.0 - up).astype(BF16), line * up.astype(BF16)]
+        made = lax.dot_general(
+            jnp.concatenate(lines, axis=0), hots, nt, preferred_element_type=F32
+        )
+        for n in range(2):
+            features = pl.ds(pl.multiple_of((i + n) * DS, DS), DS)
+            for side in range(2):
+                at_row = (2 * n + side) * 3 * DS
+                both = made[at_row:at_row + 3 * DS, n * half:(n + 1) * half]
+                positions = slice(side * half, (side + 1) * half)
+                sums_t[features, positions] = both[:DS] + both[DS:2 * DS]
+                counts_t[features, positions] = both[2 * DS:]
 
     def sum_half(df, q, h):
         f = (me_f + df) % n_feat
-        kinds = jnp.concatenate([kinds_ref[...]] * (rows // LANES), axis=1)
-        ids = [f * groups + member(h * batch + i, q) for i in range(batch)]
-        for i in range(batch):
-            hots[i * K:(i + 1) * K, :] = one_hot(codes_all[pl.ds(ids[i], 1), :], kinds)
-        full = jnp.dot(hots[...], v_ref[...], preferred_element_type=F32)
-        high = full.astype(BF16)
-        low = (full - high.astype(F32)).astype(BF16)
-        r_tile = r_tiles[f * tiles + q]
-        sums = jnp.dot(high, r_tile, preferred_element_type=F32) + jnp.dot(
-            low, r_tile, preferred_element_type=F32
-        )
-        for i in range(batch):
-            gathered[ids[i], :K] = high[i * K:(i + 1) * K]
-            gathered[ids[i], K:] = low[i * K:(i + 1) * K]
-            mine = lane // DS == h * batch + i
-            part[q, df] = jnp.where(mine, sums[i * K:(i + 1) * K], part[q, df])
-
-        @pl.when(df == 0)
+
+        def one(i, carry):
+            sum_pair(f, q, h * (PER // 2) + 2 * i)
+            return carry
+
+        lax.fori_loop(0, PER // 4, one, 0)
+
+        @pl.when(h == 1)
         def _():
-            ones = jnp.ones((LANES, LANES), BF16)
-            for i in range(batch):
-                some = hots[i * K:(i + 1) * K, :LANES]
-                for c in range(1, rows // LANES):
-                    some = some + hots[i * K:(i + 1) * K, c * LANES:(c + 1) * LANES]
-                count = jnp.dot(some, ones, preferred_element_type=F32)
-                mine = lane // DS == h * batch + i
-                part[q, n_feat] = jnp.where(mine, count, part[q, n_feat])
-
-    half, quarter = K // 2, K // 4
+            part[q, df] = sums_t[...].T
+
+            @pl.when(df == 0)
+            def _():
+                part[q, n_feat] = counts_t[...].T
 
     def core_copy(q):
         return remote(
@@ -183,17 +204,32 @@
             for s in range(1, deep)
         ]
 
+    def rebuild(q, lo):
+        def one(i, carry):
+            places, ids, lines = [], [], []
+            blank = jnp.zeros((2 * DS, half), BF16)
+            for n in range(2):
+                g = lo + 2 * i + n
+                p, e = g // per, g % per
+                gz, gx, gc = p % deep, (p // deep) % 2, p // (2 * deep)
+                r = (gz * 2 + gx) * 2 + gc
+                line = table_t[q, pl.ds(pl.multiple_of((r * per + e) * DS, DS), DS), :]
+                both = jnp.concatenate([line[:, :half], line[:, half:]], axis=0)
+                lines.append(jnp.concatenate([both, blank] if n == 0 else [blank, both], axis=1))
+                ids.append(r * owned + q * per + e)
+                places.append(pl.ds(pl.multiple_of(g * DS, DS), DS))
+            hots, uppers = pair(*ids)
+            made = jnp.dot(jnp.concatenate(lines, axis=0), hots, preferred_element_type=F32)
+            for n in range(2):
+                a = 2 * n * DS
+                chosen = jnp.where(uppers[n], made[a + DS:a + 2 * DS], made[a:a + DS])
+                recon[places[n], :] = chosen.astype(BF16)
+            return carry
+
+        lax.fori_loop(0, n_row * per // 8, one, 0)
+
     def gradient(q):
-        def one(i, carry):
-            p, e = i // per, i % per
-            gz, gx, gc = p % deep, (p // deep) % 2, p // (2 * deep)
-            r = (gz * 2 + gx) * 2 + gc
-            line = table_t[q, pl.ds(pl.multiple_of((r * per + e) * DS, DS), DS), :]
-            made = jnp.dot(line, gathered[r * owned + q * per + e], preferred_element_type=F32)
-            g_part[q, pl.ds(pl.multiple_of(i * DS, DS), DS), :] = made * inverse
-            return carry
-
-        lax.fori_loop(0, n_row * per, one, 0)
+        g_part[q] = inverse * jnp.dot(recon[...], v_ref[...], preferred_element_type=F32)
 
     def start(copies):
         for copy in copies:
@@ -240,19 +276,20 @@
         elif s == 7:
             wait(table_feat(q))
             start(table_core(q))
-        elif s == 8:
+        else:
             wait(table_core(q))
             for f in range(n_feat):
                 turned = table[q, :, f].astype(F32).reshape(K, LANES).T.astype(BF16)
-                for side in range(2):
-                    table_t[q, f * LANES:(f + 1) * LANES, side * K:(side + 1) * K] = turned
-            gradient(q)
+                table_t[q, f * LANES:(f + 1) * LANES, :] = turned
+
+    def g_stage(s, q):
+        if s == 0:
             g_core_copy(q).start()
-        elif s == 9:
+        elif s == 1:
             g_core_copy(q).wait()
             g_sum_core[q] = g_part[q, pl.ds(core * g_half, g_half)] + g_got_core[q]
             g_x_copy(q).start()
-        elif s == 10:
+        elif s == 2:
             g_x_copy(q).wait()
             g_sum_x[q] = g_sum_core[q, pl.ds(x * g_quarter, g_quarter)] + g_got_x[q]
             start(g_z_copies(q))
@@ -263,11 +300,20 @@
                 total = total + g_got_z[q, i]
             grad_ref[pl.ds(pl.multiple_of(q * deal, deal), deal), :] = total
 
-    stages = 12
     each = 2 * n_feat
     steps = tiles * each
+    stages = 9
+    after = max([steps] + [each * (q + 1) + stages - 4 * q for q in range(tiles)])
+    ends = after + 4 * tiles
 
     def step(t, carry):
+        for s in reversed(range(4)):
+            g = t - after - 4 - s
+
+            @pl.when((g >= 0) & (g % 4 == 0) & (g // 4 < tiles))
+            def _():
+                g_stage(s, g // 4)
+
         for s in reversed(range(stages)):
             g = t - each - s
 
@@ -277,11 +323,26 @@
 
         @pl.when(t < steps)
         def _():
-            sum_half((n_feat - 1) - (t % each) // 2, t // each, t % 2)
+            q = t // each
+
+            @pl.when(t % each == 0)
+            def _():
+                build(q)
+
+            sum_half((n_feat - 1) - (t % each) // 2, q, t % 2)
+
+        @pl.when((t >= after) & (t < ends))
+        def _():
+            u = t - after
+            rebuild(u // 4, (u % 4) * (n_row * per // 4))
+
+            @pl.when(u % 4 == 3)
+            def _():
+                gradient(u // 4)
 
         return carry
 
-    lax.fori_loop(0, steps + stages, step, 0)
+    lax.fori_loop(0, ends + 4, step, 0)
 
 
 def shards(vectors, rotation, codes, live_rows):
@@ -295,7 +356,9 @@
     g_rows = n_row * deal
     others, far = max(n_feat - 1, 1), max(deep - 1, 1)
     keep = jnp.arange(rows, dtype=jnp.int32) < live_rows[0]
-    coded = jnp.where(keep[:, None], codes, -1).astype(BF16).T
+    owner, inside = codes // own, codes % own
+    place = ((owner % 2 * 2 + owner // 2 % 2) * deep + owner // 4) * own + inside
+    coded = jnp.where(keep[:, None], place, -1).astype(BF16).T
     vmem = pltpu.VMEM
     sem = pltpu.SemaphoreType.DMA
     means, grad_t = pl.pallas_call(
@@ -309,10 +372,11 @@
         scratch_shapes=[
             vmem((others, groups, rows), BF16),
             vmem((n_feat * groups, rows), F32),
-            vmem((K, LANES), BF16),
-            vmem((n_feat * tiles, local, LANES), BF16),
-            vmem((PER // 2 * K, rows), BF16),
-            vmem((n_feat * groups, 2 * K, local), BF16),
+            vmem((K // 2, LANES), BF16),
+            vmem((tiles, n_feat * LANES, local), BF16),
+            vmem((n_feat * PER, 3 * DS, rows), BF16),
+            vmem((LANES, K), F32),
+            vmem((LANES, K), F32),
             vmem((tiles, n_feat + 1, K, LANES), F32),
             vmem((tiles, n_feat + 1, K // 2, LANES), F32),
             vmem((tiles, n_feat + 1, K // 2, LANES), F32),
@@ -322,7 +386,8 @@
             vmem((tiles, 2, K // 4, LANES), F32),
             vmem((tiles, far, 2, own, LANES), F32),
             vmem((tiles, 2, n_feat, 2, deep, own, LANES), BF16),
-            vmem((tiles, n_feat * LANES, 2 * K), BF16),
+            vmem((tiles, n_feat * LANES, K), BF16),
+            vmem((g_rows, rows), BF16),
             vmem((tiles, g_rows, local), F32),
             vmem((tiles, g_rows // 2, local), F32),
             vmem((tiles, g_rows // 2, local), F32),

time: 141 us -> 130 us (0.922)
  Pallas kernels: 134 us -> 123 us
    pallas_call x1, Pallas kernels: 134 us -> 123 us  [shards(): pl.pallas_call(functools.partial(kernel, n_row, n_feat, 1.0 / (rows * n_r...]
where the time goes in v4:
time: 130 us
  Pallas kernels  123 us (95%)
  local copies, waits for them, and re-layouts  3.48 us (3%)
  other arithmetic  2.54 us (2%)
  between operations  1.31 us (1%)
    pallas_call x1, Pallas kernels, shards(): pl.pallas_call(functools.partial(kernel, n_row, n_feat, 1.0 / (rows * n_r...  123 us

profile of v4, /device:TPU:0, one launch (start us, length us, event | category | flops | bytes accessed | tf_op | source)
XLA Modules:
  0.0 129.9 jit_solution(12878476675119959996)
XLA Ops:
  1.3 2.5 %fusion.15.codes_ref = bf16[32,2560]{1,0:T(8,128)(2,1)} fusion(s32[2560,32]{0,1:T(8,128)} %param.6, pred[2560]{0:T(1024)(128)(4,1)S(1)} %iota_compare_fusion), kind=kLoop, calls=%fused_computation.33 | loop fusion | flops 5488640 | bytes 494080 | tf_op jit(solution)/shard_map/transpose | solution.py:361
  3.8 122.6 %shard_map.59 = (f32[4,16,128]{2,1,0:T(8,128)}, f32[64,512]{1,0:T(8,128)}) custom-call(bf16[2560,512]{1,0:T(8,128)(2,1)} %v_ref.1, bf16[512,1024]{1,0:T(8,128)(2,1)} %r_ref.1, bf16[32,2560]{1,0:T(8,128)(2,1)} %fusion.15.codes_ref), custom_call_target="tpu_custom_call" | custom-call | tf_op jit(solution)/shard_map/pallas_call | solution.py:364
  126.4 0.9 reshape.14
  127.3 0.2 copy.6
  127.5 0.9 reshape.15
  128.3 1.6 %copy.9 = f32[64,512]{1,0:T(8,128)} copy(f32[64,512]{1,0:T(8,128)} %get-tuple-element.9) | data formatting | bytes 262144
  (1 shorter events, 0.0 us)

commit v5 on v4

--- a/solution.py
+++ b/solution.py
@@ -24,10 +24,10 @@
     n_row, n_feat, inverse,
     v_ref, r_ref, codes_ref, cent_ref, grad_ref,
     code_in, codes_all, kinds_ref, r_tiles, weights, sums_t, counts_t,
-    part, got_core, sum_core, got_feat, sum_feat, got_x, sum_x, got_z,
+    part, got_core, sum_core, got,
     table, table_t, recon,
     g_part, g_got_core, g_sum_core, g_got_x, g_sum_x, g_got_z,
-    code_sems, s_core, s_feat, s_x, s_z, t_z, t_x, t_feat, t_core, g_core, g_x, g_z,
+    code_sems, s_core, s_peer, t_peer, t_core, g_core, g_x, g_z,
 ):
     rows, local = v_ref.shape
     groups = codes_ref.shape[0]
@@ -48,10 +48,23 @@
     f_peers = [{"feat": (me_f + s) % n_feat} for s in range(1, n_feat)]
 
     barrier = pltpu.get_barrier_semaphore()
-    everyone = [sib_core, sib_x] + z_peers + f_peers
-    for peer in everyone:
-        pl.semaphore_signal(barrier, inc=1, device_id=peer, device_id_type=MESH)
-    pl.semaphore_wait(barrier, len(everyone))
+    pl.semaphore_signal(barrier, inc=1, device_id=sib_core, device_id_type=MESH)
+
+    def peer(df, n):
+        place = at((z + n % deep) % deep, (x + n // deep) % 2, core)
+        return {**place, "feat": (me_f + df) % n_feat}
+
+    def each_peer(act):
+        for df in range(n_feat):
+            def one(n, carry, df=df):
+                act(df, n)
+                return carry
+
+            lax.fori_loop(0 if df else 1, 2 * deep, one, 0)
+
+    each_peer(lambda df, n: pl.semaphore_signal(
+        barrier, inc=1, device_id=peer(df, n), device_id_type=MESH))
+    pl.semaphore_wait(barrier, 2 * deep * n_feat)
 
     def remote(src, dst, sems, peer):
         return pltpu.make_async_remote_copy(
@@ -134,53 +147,33 @@
 
         @pl.when(h == 1)
         def _():
-            part[q, df] = sums_t[...].T
+            part[q, df + 1] = sums_t[...].T
 
             @pl.when(df == 0)
             def _():
-                part[q, n_feat] = counts_t[...].T
+                part[q, 0] = counts_t[...].T
 
     def core_copy(q):
         return remote(
             part.at[q, :, pl.ds((1 - core) * half, half)], got_core.at[q], s_core.at[q], sib_core
         )
 
-    def feat_copies(q):
-        return [
-            remote(sum_core.at[q, s], got_feat.at[q, s - 1], s_feat.at[q, s - 1], f_peers[s - 1])
-            for s in range(1, n_feat)
-        ]
-
-    def x_copy(q):
+    def peer_copy(q, df, n):
+        px, pz = (x + n // deep) % 2, (z + n % deep) % deep
+        piece = pl.ds((px * deep + pz) * own, own)
+        slabs = pl.ds(df + 1, 1) if df else pl.ds(0, 2)
+        lands = pl.ds(1, 1) if df else pl.ds(0, 2)
         return remote(
-            sum_feat.at[q, :, pl.ds((1 - x) * quarter, quarter)], got_x.at[q], s_x.at[q], sib_x
-        )
-
-    def z_copies(q):
-        return [
-            remote(
-                sum_x.at[q, :, pl.ds(((z + s) % deep) * own, own)], got_z.at[q, s - 1],
-                s_z.at[q, s - 1], z_peers[s - 1],
-            )
-            for s in range(1, deep)
-        ]
-
-    def same(piece, sems, peer):
-        return remote(piece, piece, sems, peer)
-
-    def table_z(q):
+            sum_core.at[q, slabs, piece], got.at[q, df, n, lands], s_peer.at[q, df, n], peer(df, n)
+        )
+
+    def table_copy(q, df, n):
         piece = table.at[q, core, me_f, x, z]
-        return [same(piece, t_z.at[q, s], z_peers[s]) for s in range(deep - 1)]
-
-    def table_x(q):
-        return [same(table.at[q, core, me_f, x], t_x.at[q], sib_x)]
-
-    def table_feat(q):
-        piece = table.at[q, core, me_f]
-        return [same(piece, t_feat.at[q, s], f_peers[s]) for s in range(n_feat - 1)]
+        return remote(piece, piece, t_peer.at[q, df, n], peer(df, n))
 
     def table_core(q):
-        return [same(table.at[q, core], t_core.at[q], sib_core)]
+        piece = table.at[q, core]
+        return remote(piece, piece, t_core.at[q], sib_core)
 
     deal = per * DS
     g_half, g_quarter = n_row * deal // 2, n_row * deal // 4
@@ -245,39 +238,25 @@
         elif s == 1:
             core_copy(q).wait()
             sum_core[q] = part[q, :, pl.ds(core * half, half)] + got_core[q]
-            start(feat_copies(q))
+            each_peer(lambda df, n: peer_copy(q, df, n).start())
         elif s == 2:
-            wait(feat_copies(q))
-            total = sum_core[q, 0]
-            for i in range(n_feat - 1):
-                total = total + got_feat[q, i]
-            sum_feat[q, 0] = total
-            sum_feat[q, 1] = sum_core[q, n_feat]
-            x_copy(q).start()
-        elif s == 3:
-            x_copy(q).wait()
-            sum_x[q] = sum_feat[q, :, pl.ds(x * quarter, quarter)] + got_x[q]
-            start(z_copies(q))
-        elif s == 4:
-            wait(z_copies(q))
-            total = sum_x[q, :, pl.ds(z * own, own)]
-            for i in range(deep - 1):
-                total = total + got_z[q, i]
-            mean = total[0] / (total[1] + 1.0)
+            each_peer(lambda df, n: peer_copy(q, df, n).wait())
+            mine = pl.ds((x * deep + z) * own, own)
+            count, total = sum_core[q, 0, mine], sum_core[q, 1, mine]
+            for df in range(n_feat):
+                for n in range(0 if df else 1, 2 * deep):
+                    total = total + got[q, df, n, 1]
+                    if df == 0:
+                        count = count + got[q, df, n, 0]
+            mean = total / (count + 1.0)
             cent_ref[q] = mean
             table[q, core, me_f, x, z] = mean.astype(BF16)
-            start(table_z(q))
-        elif s == 5:
-            wait(table_z(q))
-            start(table_x(q))
-        elif s == 6:
-            wait(table_x(q))
-            start(table_feat(q))
-        elif s == 7:
-            wait(table_feat(q))
-            start(table_core(q))
+            each_peer(lambda df, n: table_copy(q, df, n).start())
+        elif s == 3:
+            each_peer(lambda df, n: table_copy(q, df, n).wait())
+            table_core(q).start()
         else:
-            wait(table_core(q))
+            table_core(q).wait()
             for f in range(n_feat):
                 turned = table[q, :, f].astype(F32).reshape(K, LANES).T.astype(BF16)
                 table_t[q, f * LANES:(f + 1) * LANES, :] = turned
@@ -302,20 +281,20 @@
 
     each = 2 * n_feat
     steps = tiles * each
-    stages = 9
-    after = max([steps] + [each * (q + 1) + stages - 4 * q for q in range(tiles)])
+    stages, gap = 5, 3
+    after = max([steps] + [each * (q + 1) + gap * (stages - 1) - 4 * q for q in range(tiles)])
     ends = after + 4 * tiles
 
     def step(t, carry):
         for s in reversed(range(4)):
-            g = t - after - 4 - s
+            g = t - after - 4 - gap * s
 
             @pl.when((g >= 0) & (g % 4 == 0) & (g // 4 < tiles))
             def _():
                 g_stage(s, g // 4)
 
         for s in reversed(range(stages)):
-            g = t - each - s
+            g = t - each - gap * s
 
             @pl.when((g >= 0) & (g % each == 0) & (g // each < tiles))
             def _():
@@ -342,7 +321,7 @@
 
         return carry
 
-    lax.fori_loop(0, ends + 4, step, 0)
+    lax.fori_loop(0, ends + 1 + 3 * gap, step, 0)
 
 
 def shards(vectors, rotation, codes, live_rows):
@@ -380,11 +359,7 @@
             vmem((tiles, n_feat + 1, K, LANES), F32),
             vmem((tiles, n_feat + 1, K // 2, LANES), F32),
             vmem((tiles, n_feat + 1, K // 2, LANES), F32),
-            vmem((tiles, others, K // 2, LANES), F32),
-            vmem((tiles, 2, K // 2, LANES), F32),
-            vmem((tiles, 2, K // 4, LANES), F32),
-            vmem((tiles, 2, K // 4, LANES), F32),
-            vmem((tiles, far, 2, own, LANES), F32),
+            vmem((tiles, n_feat, 2 * deep, 2, own, LANES), F32),
             vmem((tiles, 2, n_feat, 2, deep, own, LANES), BF16),
             vmem((tiles, n_feat * LANES, K), BF16),
             vmem((g_rows, rows), BF16),
@@ -396,12 +371,8 @@
             vmem((tiles, far, deal, local), F32),
             sem((others, 2)),
             sem((tiles, 2)),
-            sem((tiles, others, 2)),
-            sem((tiles, 2)),
-            sem((tiles, far, 2)),
-            sem((tiles, far, 2)),
-            sem((tiles, 2)),
-            sem((tiles, others, 2)),
+            sem((tiles, n_feat, 2 * deep, 2)),
+            sem((tiles, n_feat, 2 * deep, 2)),
             sem((tiles, 2)),
             sem((tiles, 2)),
             sem((tiles, 2)),

time: 130 us -> 90.2 us (0.69)
  Pallas kernels: 123 us -> 82.6 us
    pallas_call x1, Pallas kernels: 123 us -> 82.6 us  [shards(): pl.pallas_call(functools.partial(kernel, n_row, n_feat, 1.0 / (rows * n_r...]
where the time goes in v5:
time: 90.2 us; the launch traced here: 89.9 us
  Pallas kernels  82.6 us (92%)
  local copies, waits for them, and re-layouts  3.48 us (4%)
  other arithmetic  2.54 us (3%)
  between operations  1.31 us (1%)
    pallas_call x1, Pallas kernels, shards(): pl.pallas_call(functools.partial(kernel, n_row, n_feat, 1.0 / (rows * n_r...  82.6 us
    transpose x1, other arithmetic, shards(): coded = jnp.where(keep[:, None], place, -1).astype(BF16).T  2.53 us

profile of v5, /device:TPU:0, one launch (start us, length us, event | category | flops | bytes accessed | tf_op | source)
XLA Modules:
  0.0 89.9 jit_solution(13566699246368779323)
XLA Ops:
  1.3 2.5 %fusion.15.codes_ref = bf16[32,2560]{1,0:T(8,128)(2,1)} fusion(s32[2560,32]{0,1:T(8,128)} %param.6, pred[2560]{0:T(1024)(128)(4,1)S(1)} %iota_compare_fusion), kind=kLoop, calls=%fused_computation.33 | loop fusion | flops 5488640 | bytes 494080 | tf_op jit(solution)/shard_map/transpose | solution.py:340
  3.8 82.6 %shard_map.59 = (f32[4,16,128]{2,1,0:T(8,128)}, f32[64,512]{1,0:T(8,128)}) custom-call(bf16[2560,512]{1,0:T(8,128)(2,1)} %v_ref.1, bf16[512,1024]{1,0:T(8,128)(2,1)} %r_ref.1, bf16[32,2560]{1,0:T(8,128)(2,1)} %fusion.15.codes_ref), custom_call_target="tpu_custom_call" | custom-call | tf_op jit(solution)/shard_map/pallas_call | solution.py:343
  86.4 0.9 reshape.14
  87.3 0.2 copy.6
  87.5 0.9 reshape.15
  88.3 1.6 %copy.9 = f32[64,512]{1,0:T(8,128)} copy(f32[64,512]{1,0:T(8,128)} %get-tuple-element.9) | data formatting | bytes 262144
  (1 shorter events, 0.0 us)

commit v6 on v5

--- a/solution.py
+++ b/solution.py
@@ -143,7 +143,7 @@
             sum_pair(f, q, h * (PER // 2) + 2 * i)
             return carry
 
-        lax.fori_loop(0, PER // 4, one, 0)
+        lax.fori_loop(0, PER // 4, one, 0, unroll=True)
 
         @pl.when(h == 1)
         def _():
@@ -219,7 +219,7 @@
                 recon[places[n], :] = chosen.astype(BF16)
             return carry
 
-        lax.fori_loop(0, n_row * per // 8, one, 0)
+        lax.fori_loop(0, n_row * per // 8, one, 0, unroll=2)
 
     def gradient(q):
         g_part[q] = inverse * jnp.dot(recon[...], v_ref[...], preferred_element_type=F32)

time: 90.2 us -> 87.6 us (0.971)
  Pallas kernels: 82.6 us -> 80 us
    pallas_call x1, Pallas kernels: 82.6 us -> 80 us  [shards(): pl.pallas_call(functools.partial(kernel, n_row, n_feat, 1.0 / (rows * n_r...]
where the time goes in v6:
time: 87.6 us; the launch traced here: 87.3 us
  Pallas kernels  80 us (91%)
  local copies, waits for them, and re-layouts  3.48 us (4%)
  other arithmetic  2.54 us (3%)
  between operations  1.31 us (1%)
    pallas_call x1, Pallas kernels, shards(): pl.pallas_call(functools.partial(kernel, n_row, n_feat, 1.0 / (rows * n_r...  80 us
    transpose x1, other arithmetic, shards(): coded = jnp.where(keep[:, None], place, -1).astype(BF16).T  2.53 us

profile of v6, /device:TPU:0, one launch (start us, length us, event | category | flops | bytes accessed | tf_op | source)
XLA Modules:
  0.0 87.3 jit_solution(808525335573168334)
XLA Ops:
  1.3 2.5 %fusion.15.codes_ref = bf16[32,2560]{1,0:T(8,128)(2,1)} fusion(s32[2560,32]{0,1:T(8,128)} %param.6, pred[2560]{0:T(1024)(128)(4,1)S(1)} %iota_compare_fusion), kind=kLoop, calls=%fused_computation.33 | loop fusion | flops 5488640 | bytes 494080 | tf_op jit(solution)/shard_map/transpose | solution.py:340
  3.8 80.0 %shard_map.59 = (f32[4,16,128]{2,1,0:T(8,128)}, f32[64,512]{1,0:T(8,128)}) custom-call(bf16[2560,512]{1,0:T(8,128)(2,1)} %v_ref.1, bf16[512,1024]{1,0:T(8,128)(2,1)} %r_ref.1, bf16[32,2560]{1,0:T(8,128)(2,1)} %fusion.15.codes_ref), custom_call_target="tpu_custom_call" | custom-call | tf_op jit(solution)/shard_map/pallas_call | solution.py:343
  83.8 0.9 %reshape.14 = f32[4,16,8,1,16]{4,2,1,0,3:T(8,128)S(1)} reshape(f32[4,16,128]{2,1,0:T(8,128)} %get-tuple-element.4) | data formatting | bytes 65536 | tf_op jit(solution)/shard_map/reshape | solution.py:385
  84.7 0.2 copy.6
  84.9 0.9 reshape.15
  85.7 1.6 %copy.9 = f32[64,512]{1,0:T(8,128)} copy(f32[64,512]{1,0:T(8,128)} %get-tuple-element.9) | data formatting | bytes 262144
  (1 shorter events, 0.0 us)
